TPU v7x, 32 devices: a whole 2x2x4 slice. The times are simulated.
32 devices in a mesh: seq: 8 (over z, x), exp: 4 (over y, core).
Axes of the slice: x: 2, y: 2, z: 4, core: 2. Of those that a mesh axis runs over, the one named last changes fastest.
Arguments:
- residual_in: bfloat16 [4, 2048, 2048], P('exp', 'seq'), may hold values from -6 to 6
- query_matrix: bfloat16 [4, 2048, 2048], P('exp', 'seq'), may hold values from -6 to 6
- key_vectors: bfloat16 [4, 2048, 2048], P('exp', 'seq'), may hold values from -6 to 6
- value_vectors: bfloat16 [4, 2048, 2048], P('exp', 'seq'), may hold values from -6 to 6
- head_gain: float32 [2048], replicated, may hold values from 0.5 to 1.5
- norm_gain: float32 [2048], replicated, may hold values from 0.5 to 1.5
- expert_ids: int32 [4, 2048, 4], P('exp', 'seq'), may hold values from 0 to 7, all different within a row; in each aligned block of 256 rows (0 to 255, 256 to 511, ..., all dimensions but the last counted through in order) at most 192 rows name the same one
- gate_probs: float32 [4, 2048, 4], P('exp', 'seq'), may hold values from 0.25 to 1
- w_gate: bfloat16 [8, 2048, 1408], P('exp'), may hold values from -0.125 to 0.125
- w_up: bfloat16 [8, 2048, 1408], P('exp'), may hold values from -0.125 to 0.125
- w_down: bfloat16 [8, 1408, 2048], P('exp'), may hold values from -0.15625 to 0.15625
Outputs:
- layer_out: bfloat16 [4, 2048, 2048], P('exp', 'seq')
Inputs may be any that keep to these rules, and one draw needn't show every extreme that they name: `expert_ids`: the 4 experts of one position differ; among the 256 positions of one device, no expert is named by more than 192 routes.
All inputs are finite; a program needn't handle non-finite values.
Results may differ from a plain program's by a relative error of at most 0.013.
Values may be sent and summed in bfloat16 or wider, within the bound.
A program may use at most 128 MiB of HBM per device.

v0:
```python
import jax
import jax.numpy as jnp
from jax import lax
from jax.sharding import PartitionSpec as P

D = 2048
HEADS = 16
HD = 128
TOP = 4
EXPERTS = 8
CAP = 192


def on_device(
    residual_in,
    query_matrix,
    key_vectors,
    value_vectors,
    head_gain,
    norm_gain,
    expert_ids,
    gate_probs,
    w_gate,
    w_up,
    w_down,
):
    positions = residual_in.shape[1]
    queries = query_matrix[0].reshape(positions, HEADS, HD)
    key_rows = key_vectors[0].reshape(positions, HEADS, HD)
    value_rows = value_vectors[0].reshape(positions, HEADS, HD)
    state = jnp.einsum("thd,the->hde", key_rows, value_rows, preferred_element_type=jnp.float32)
    my_index = lax.axis_index("seq")
    piece = lax.all_gather(state[None], "seq", axis=0, tiled=True)
    owners = jnp.arange(piece.shape[0], dtype=jnp.int32)
    earlier = owners < my_index
    prefix = jnp.sum(jnp.where(earlier[:, None, None, None], piece, 0.0), axis=0)
    causal = jnp.tril(jnp.ones((positions, positions), dtype=bool))
    scores = jnp.einsum("thd,uhd->htu", queries, key_rows, preferred_element_type=jnp.float32)
    weights = jnp.where(causal[None], scores, 0.0).astype(jnp.bfloat16)
    inner = jnp.einsum("htu,uhd->thd", weights, value_rows, preferred_element_type=jnp.float32)
    outer_product = jnp.einsum(
        "thd,hde->the", queries, prefix.astype(jnp.bfloat16), preferred_element_type=jnp.float32
    )
    mixed = inner + outer_product
    mean_square = jnp.mean(mixed * mixed, axis=-1, keepdims=True)
    attn = (mixed * lax.rsqrt(mean_square + 1e-06)).reshape(positions, D) * head_gain
    resid_float = (
        (residual_in[0].astype(jnp.float32) + attn).astype(jnp.bfloat16).astype(jnp.float32)
    )
    row_square = jnp.mean(resid_float * resid_float, axis=-1, keepdims=True)
    normed = (resid_float * lax.rsqrt(row_square + 1e-06) * norm_gain).astype(jnp.bfloat16)
    route_ids = expert_ids[0].reshape(-1)
    route_gates = gate_probs[0]
    expert_indicator = (route_ids[:, None] == jnp.arange(EXPERTS, dtype=jnp.int32)[None, :]).astype(
        jnp.int32
    )
    slots = jnp.sum(
        (jnp.cumsum(expert_indicator, axis=0) - expert_indicator) * expert_indicator, axis=1
    )
    target = route_ids * CAP + slots
    token_of = jnp.arange(positions * TOP, dtype=jnp.int32) // TOP
    outgoing = (
        jnp.zeros((EXPERTS * CAP, D), jnp.bfloat16)
        .at[target]
        .set(normed[token_of])
        .reshape(EXPERTS, CAP, D)
    )
    local_count = w_gate.shape[0]
    groups = EXPERTS // local_count
    block = lax.all_to_all(outgoing, "exp", split_axis=0, concat_axis=0, tiled=True)
    count = block.shape[1]
    grouped = block.reshape(groups, local_count, count, D)
    gate_part = jnp.einsum("gend,edf->genf", grouped, w_gate, preferred_element_type=jnp.float32)
    up_part = jnp.einsum("gend,edf->genf", grouped, w_up, preferred_element_type=jnp.float32)
    hidden = (jax.nn.silu(gate_part) * up_part).astype(jnp.bfloat16)
    result = jnp.einsum("genf,efd->gend", hidden, w_down, preferred_element_type=jnp.float32)
    result = result.astype(jnp.bfloat16).reshape(EXPERTS, count, D)
    returned = lax.all_to_all(result, "exp", split_axis=0, concat_axis=0, tiled=True)
    picked = returned.reshape(EXPERTS * CAP, D)[target].reshape(positions, TOP, D)
    combined = jnp.sum(picked.astype(jnp.float32) * route_gates[:, :, None], axis=1)
    return (resid_float + combined).astype(jnp.bfloat16)[None]


def solution(mesh):
    in_specs = (
        P("exp", "seq", None),
        P("exp", "seq", None),
        P("exp", "seq", None),
        P("exp", "seq", None),
        P(),
        P(),
        P("exp", "seq", None),
        P("exp", "seq", None),
        P("exp", None, None),
        P("exp", None, None),
        P("exp", None, None),
    )
    out_specs = P("exp", "seq", None)
    return jax.shard_map(
        on_device, mesh=mesh, in_specs=in_specs, out_specs=out_specs, check_vma=False
    )
```

profile of v0, /device:TPU:24, one launch (start us, length us, event | category | flops | bytes accessed | tf_op | source)
XLA Modules:
  0.0 414.6 jit_solution(7338317783509641407)
XLA Ops:
  6.5 1.5 copy.51
  8.0 1.5 copy.53
  9.5 1.4 fusion.28
  11.4 1.5 copy.52
  12.8 2.3 reduce-window.6
  16.0 2.8 fusion.26
  18.8 116.3 %all-gather.3.cloned.1.call-done = f32[128,128,128]{2,1,0:T(8,128)} async-done(((f32[16,128,128]{2,1,0:T(8,128)}), f32[128,128,128]{2,1,0:T(8,128)}) %all-gather.3.cloned.1.call-update) | async-done | bytes 8388624 | tf_op jit(solution)/shard_map/all_gather | solution.py:33
  135.1 4.5 %select_reduce_fusion = bf16[16,128,128]{2,1,0:T(8,128)(2,1)S(1)} fusion(f32[8,16,128,128]{3,2,1,0:T(8,128)} %bitcast.103, pred[8]{0:T(512)(128)(4,1)S(1)} %iota_compare_fusion.3), kind=kLoop, calls=%fused_computation.17 | loop fusion | flops 3932160 | bytes 8912904 | tf_op jit(solution)/shard_map/reduce_sum | solution.py:36
  139.6 1.9 multiply_reduce_fusion.1
  141.7 1.9 copy.42
  143.6 2.1 fusion.22
  147.0 22.9 %scatter_custom_fusion = bf16[1536,2048]{1,0:T(8,128)(2,1)} fusion(s32[1024]{0:T(1024)S(1)} %bitcast.115, bf16[256,2048]{1,0:T(8,128)(2,1)} %fusion.24, s32[1024]{0:T(1024)S(1)} %broadcast_clamp_fusion.1, bf16[]{:T(256)} %constant.44.clone.1), kind=kCustom, calls=%fused_computation.21 | custom fusion | bytes 6291968 | tf_op jit(solution)/shard_map/scatter | solution.py:65
  169.9 74.6 %all_to_all.10 = bf16[8,192,2048]{2,1,0:T(8,128)(2,1)S(1)} all-to-all(bf16[8,192,2048]{2,1,0:T(8,128)(2,1)} %bitcast.100), channel_id=1, replica_groups=mesh['seq'=8,'exp'=4] {'exp'}, dimensions={0} | all-to-all | bytes 12582912 | tf_op jit(solution)/shard_map/all_to_all | solution.py:70
  244.5 2.6 copy-done.1
  247.1 14.7 %fusion.2 = f32[2,4,192,1408]{3,2,1,0:T(8,128)} fusion(bf16[2,2048,1408]{2,1,0:T(8,128)(2,1)} %param.20, bf16[4,2,192,2048]{3,2,1,0:T(8,128)(2,1)S(1)} %bitcast.104), kind=kOutput, calls=%fused_computation.5 | convolution fusion | flops 8858370048 | bytes 26476544 | tf_op jit(solution)/shard_map/gend,edf->genf/dot_general | solution.py:74
  261.8 28.0 %convert_bitcast_fusion = bf16[4,2,192,2048]{3,2,0,1:T(8,128)(2,1)} fusion(bf16[2,1408,2048]{2,1,0:T(8,128)(2,1)} %param.21, f32[2,4,192,1408]{3,2,1,0:T(8,128)} %fusion.2, bf16[2,2048,1408]{2,1,0:T(8,128)(2,1)} %param.19, bf16[4,2,192,2048]{3,2,1,0:T(8,128)(2,1)} %bitcast.105), kind=kOutput, calls=%fused_computation.18 | convolution fusion | flops 17732861952 | bytes 44302336 | tf_op jit(solution)/shard_map/genf,efd->gend/dot_general | solution.py:76
  289.8 6.5 %copy.45 = bf16[4,2,192,2048]{3,2,1,0:T(8,128)(2,1)} copy(bf16[4,2,192,2048]{3,2,0,1:T(8,128)(2,1)} %convert_bitcast_fusion) | data formatting | bytes 12582912 | tf_op jit(solution)/shard_map/convert_element_type | solution.py:77
  296.3 5.6 %all-to-all-start.1 = ((bf16[8,192,2048]{2,1,0:T(8,128)(2,1)}), bf16[8,192,2048]{2,1,0:T(8,128)(2,1)}, u32[]{:S(2)}, u32[]{:S(2)}) async-start(bf16[8,192,2048]{2,1,0:T(8,128)(2,1)} %bitcast.99), calls=%async_computation.1 | async-start | bytes 12582912 | tf_op jit(solution)/shard_map/all_to_all | solution.py:78
  302.1 1.9 copy.38
  304.0 68.4 %all-to-all-done.1 = bf16[8,192,2048]{2,1,0:T(8,128)(2,1)} async-done(((bf16[8,192,2048]{2,1,0:T(8,128)(2,1)}), bf16[8,192,2048]{2,1,0:T(8,128)(2,1)}, u32[]{:S(2)}, u32[]{:S(2)}) %all-to-all-start.1) | async-done | bytes 6291488 | tf_op jit(solution)/shard_map/all_to_all | solution.py:78
  372.4 12.4 %gather_fusion = bf16[1024,2048]{1,0:T(8,128)(2,1)} fusion(bf16[1536,2048]{1,0:T(8,128)(2,1)} %bitcast.22, s32[1024]{0:T(1024)S(1)} %broadcast_clamp_fusion), kind=kCustom, calls=%fused_computation.1 | custom fusion | bytes 8392704 | tf_op jit(solution)/shard_map/gather | solution.py:79
  384.8 8.3 %reshape.180 = f32[256,4,2048]{2,1,0:T(4,128)} reshape(bf16[1024,2048]{1,0:T(8,128)(2,1)} %gather_fusion) | data formatting | bytes 12582912 | tf_op jit(solution)/shard_map/convert_element_type | solution.py:80
  393.1 11.5 %multiply_reduce_fusion = f32[256,2048]{1,0:T(8,128)} fusion(f32[256,4,2048]{2,1,0:T(4,128)} %reshape.180, f32[256,4]{1,0:T(8,128)S(1)} %copy.46), kind=kLoop, calls=%fused_computation.16 | loop fusion | flops 3670016 | bytes 10489856 | tf_op jit(solution)/shard_map/reduce_sum | solution.py:80
  404.6 3.1 fusion.25
  (41 shorter events, 2.9 us)
Async XLA Ops:
  6.5 4.4 %copy-start.6 = (s32[1,256,4]{1,2,0:T(4,128)S(1)}, s32[1,256,4]{1,2,0:T(4,128)}, u32[]{:S(2)}) copy-start(s32[1,256,4]{1,2,0:T(4,128)} %param.17) | copy-start | bytes 12292
  6.5 128.6 %all-gather.3.cloned.1.call-start = ((), (), s32[]{:S(2)}) async-start(), calls=%async_computation.2 | async-start | bytes 9437184 | tf_op jit(solution)/shard_map/all_gather | solution.py:33
  12.8 122.3 %copy-start.3 = (bf16[32,8,16,128]{3,2,1,0:T(8,128)(2,1)}, bf16[32,8,16,128]{3,2,1,0:T(8,128)(2,1)S(1)}, u32[]{:S(2)}) copy-start(bf16[32,8,16,128]{3,2,1,0:T(8,128)(2,1)S(1)} %copy.52) | copy-start | bytes 3145732
  18.8 120.8 %copy-start.4 = (f32[16,256,128]{1,2,0:T(8,128)S(1)}, f32[16,256,128]{1,2,0:T(8,128)}, u32[]{:S(2)}) copy-start(f32[16,256,128]{1,2,0:T(8,128)} %fusion.26) | copy-start | bytes 6291460
  139.6 4.0 copy-start.2
  139.6 4.0 copy-start.5
  141.5 4.2 %copy-start.7 = (f32[2048]{0:T(1024)S(1)}, f32[2048]{0:T(1024)}, u32[]{:S(2)}) copy-start(f32[2048]{0:T(1024)} %param.16) | copy-start | bytes 24580
  244.5 2.6 copy-start.1
  296.3 5.6 %copy-start.8 = (f32[1,256,4]{1,2,0:T(4,128)S(1)}, f32[1,256,4]{1,2,0:T(4,128)}, u32[]{:S(2)}) copy-start(f32[1,256,4]{1,2,0:T(4,128)} %param.18) | copy-start | bytes 12292
  296.3 76.1 %all-to-all-start.1 = ((bf16[8,192,2048]{2,1,0:T(8,128)(2,1)}), bf16[8,192,2048]{2,1,0:T(8,128)(2,1)}, u32[]{:S(2)}, u32[]{:S(2)}) async-start(bf16[8,192,2048]{2,1,0:T(8,128)(2,1)} %bitcast.99), calls=%async_computation.1 | async-start | bytes 12582912 | tf_op jit(solution)/shard_map/all_to_all | solution.py:78
  393.1 11.5 %copy-start = (f32[1,256,2048]{2,1,0:T(8,128)S(1)}, f32[1,256,2048]{2,1,0:T(8,128)}, u32[]{:S(2)}) copy-start(f32[1,256,2048]{2,1,0:T(8,128)} %copy.38) | copy-start | bytes 6291460
Sparse Core Ops, SparseCore 0:
  11.1 123.9 all-gather.2
where the time goes:
time: 419 us; the launch traced here: 415 us
  waiting for transfers between devices  185 us (44%)
  blocking collectives  74.6 us (18%)
  local copies, waits for them, and re-layouts  61.9 us (15%)
  matrix products  48.9 us (12%)
  other arithmetic  25.2 us (6%)
  between operations  13.6 us (3%)
  starting transfers between devices  5.63 us (1%)
    all_gather x1, waiting for transfers between devices, on_device(): piece = lax.all_gather(state[None], 'seq', axis=0, tiled=True)  116 us
    all_to_all x1, blocking collectives, on_device(): lax.all_to_all(outgoing, 'exp', split_axis=0, concat_axis=0, tiled=True)  74.6 us
    all_to_all x1, waiting for transfers between devices, on_device(): lax.all_to_all(result, 'exp', split_axis=0, concat_axis=0, tiled=True)  68.4 us
    dot_general x1, matrix products, on_device(): jnp.einsum('genf,efd->gend', hidden, w_down, preferred_element_type=jnp.f...  28 us
    scatter x1, local copies, waits for them, and re-layouts, on_device(): outgoing = jnp.zeros((EXPERTS * CAP, D), jnp.bfloat16).at[target].set(nor...  22.9 us
    dot_general x1, matrix products, on_device(): jnp.einsum('gend,edf->genf', grouped, w_up, preferred_element_type=jnp.fl...  14.7 us
    gather x1, local copies, waits for them, and re-layouts, on_device(): returned.reshape(EXPERTS * CAP, D)[target].reshape(positions, TOP, D)  12.4 us
    reduce_sum x1, other arithmetic, on_device(): jnp.sum(picked.astype(jnp.float32) * route_gates[:, :, None], axis=1)  11.5 us
  transfers between devices with their start and end apart: 2, of which 2 were waited for; matrix products, arithmetic and copies ran while one was open for 2% of the time, Pallas kernels for 0%

commit v1 on v0

v1 whole, which is shorter than its diff:
```python
import functools

import jax
import jax.numpy as jnp
from jax import lax
from jax.experimental import pallas as pl
from jax.experimental.pallas import tpu as pltpu
from jax.sharding import PartitionSpec as P

HEADS = 16
HD = 128
EXPERTS = 8
CH = 2
NCH = HEADS // CH
ROWCH = 2
TN = 512
FT = 256
MESH = pl.DeviceIdType.MESH
BF = jnp.bfloat16
F32 = jnp.float32


def dot(a, b):
    return jnp.dot(a, b, preferred_element_type=F32)


def kernel(
    cfg, res, q, k, v, hg, ng, ids, probs, wg, wu, wd, out,
    st, stb, xb, zb, zo, acc, rs, sq, gall, xall, wgv, wuv, wdv, hid, gc, to,
    lsb, lrb, rsb, rrb, rown, ysb, yrb,
    wsem, gs, gr, xs, xr, zs, zr, ys, yr, ss, sr, ls, lr, ps, pr, bs, br,
):
    n_seq, n_exp, X, L, T, D, FF = cfg
    Z = n_seq // X
    Y = n_exp // 2
    NT = D // TN
    me_s = lax.axis_index("seq")
    me_e = lax.axis_index("exp")
    z = me_s // X
    x = me_s % X
    y = me_e // 2
    c = me_e % 2
    sib = y * 2 + 1 - c

    barrier = pltpu.get_barrier_semaphore()
    for d in range(1, X):
        pl.semaphore_signal(
            barrier, inc=1, device_id={"seq": z * X + (x + d) % X}, device_id_type=MESH
        )
    for d in range(1, n_exp):
        pl.semaphore_signal(
            barrier, inc=1, device_id={"exp": (me_e + d) % n_exp}, device_id_type=MESH
        )

    @pl.when(z > 0)
    def _():
        pl.semaphore_signal(barrier, inc=1, device_id={"seq": me_s - X}, device_id_type=MESH)

    @pl.when(z < Z - 1)
    def _():
        pl.semaphore_signal(barrier, inc=1, device_id={"seq": me_s + X}, device_id_type=MESH)

    wcopies = []
    for l in range(L):
        wcopies.append(pltpu.make_async_copy(wg.at[l], wgv.at[l], wsem.at[3 * l]))
        wcopies.append(pltpu.make_async_copy(wu.at[l], wuv.at[l], wsem.at[3 * l + 1]))
    for l in range(L):
        wcopies.append(
            pltpu.make_async_copy(
                wd.at[pl.ds(l * FF, FF)], wdv.at[pl.ds(l * FF, FF)], wsem.at[3 * l + 2]
            )
        )
    for w in wcopies:
        w.start()

    lane = lax.broadcasted_iota(jnp.int32, (T, HD), 1)
    g = jnp.zeros((T, HD), F32)
    for t in range(ids.shape[1]):
        g = g + jnp.where(lane == ids[:, t : t + 1], probs[:, t : t + 1], 0.0)
    gall[me_e] = g.T[:EXPERTS]

    @pl.when(z == 0)
    def _():
        zb[...] = jnp.zeros_like(zb)

    pl.semaphore_wait(
        barrier,
        X - 1 + n_exp - 1 + jnp.where(z > 0, 1, 0) + jnp.where(z < Z - 1, 1, 0),
    )

    def remote(src, dst, send, recv, where):
        return pltpu.make_async_remote_copy(
            src_ref=src, dst_ref=dst, send_sem=send, recv_sem=recv,
            device_id=where, device_id_type=MESH,
        )

    def gcopy(d, owner):
        return remote(
            gall.at[owner], gall.at[owner], gs.at[d - 1], gr.at[d - 1],
            {"exp": (me_e + d) % n_exp},
        )

    def xcopy(d, i):
        sl = pl.ds(i * CH, CH)
        return remote(
            stb.at[sl], xb.at[d - 1, sl], xs.at[d - 1, i], xr.at[d - 1, i],
            {"seq": z * X + (x + d) % X},
        )

    def zcopy(i):
        sl = pl.ds(i * CH, CH)
        return remote(
            zo.at[sl], zb.at[sl], zs.at[i], zr.at[i],
            {"seq": jnp.minimum(me_s + X, n_seq - 1)},
        )

    for d in range(1, n_exp):
        gcopy(d, me_e).start()

    def cols_of(h):
        return pl.ds(pl.multiple_of(h * HD, HD), HD)

    def state_body(i, carry):
        for hh in range(CH):
            h = i * CH + hh
            cols = cols_of(h)
            s = lax.dot_general(
                k[:, cols], v[:, cols], (((0,), (0,)), ((), ())), preferred_element_type=F32
            )
            st[h] = s
            stb[h] = s.astype(BF)
        for d in range(1, X):
            xcopy(d, i).start()
        return carry

    lax.fori_loop(0, NCH, state_body, 0)

    sq[...] = jnp.zeros_like(sq)
    causal = lax.broadcasted_iota(jnp.int32, (T, T), 0) >= lax.broadcasted_iota(
        jnp.int32, (T, T), 1
    )

    def inner_body(i, carry):
        for hh in range(CH):
            cols = cols_of(i * CH + hh)
            s = lax.dot_general(
                q[:, cols], k[:, cols], (((1,), (1,)), ((), ())), preferred_element_type=F32
            )
            w = jnp.where(causal, s, 0.0).astype(BF)
            acc[:, cols] = dot(w, v[:, cols])
        return carry

    lax.fori_loop(0, NCH, inner_body, 0)

    def chain_body(i, carry):
        sl = pl.ds(i * CH, CH)
        t = st[sl]
        before = jnp.zeros_like(t)
        for d in range(1, X):
            xcopy(d, i).wait_recv()
            r = xb[d - 1, sl].astype(F32)
            t = t + r
            before = before + jnp.where(x >= d, r, 0.0)

        @pl.when(z > 0)
        def _():
            zcopy(i).wait_recv()

        p = zb[sl].astype(F32)

        @pl.when(z < Z - 1)
        def _():
            zo[sl] = (p + t).astype(BF)
            zcopy(i).start()

        pf = (p + before).astype(BF)
        for hh in range(CH):
            cols = cols_of(i * CH + hh)
            m = acc[:, cols] + dot(q[:, cols], pf[hh])
            ms = jnp.mean(m * m, axis=-1, keepdims=True)
            a = m * lax.rsqrt(ms + 1e-06) * hg[:, cols]
            r = (res[:, cols].astype(F32) + a).astype(BF)
            rs[:, cols] = r
            rf = r.astype(F32)
            sq[...] += rf * rf
        return carry

    lax.fori_loop(0, NCH, chain_body, 0)

    RC = T // ROWCH

    def block_rows(owner, r):
        return pl.ds(pl.multiple_of(owner * T + r * RC, RC), RC)

    def ycopy(dy, r, owner):
        rows = block_rows(owner, r)
        return remote(
            xall.at[rows], xall.at[rows], ys.at[dy - 1, r], yr.at[dy - 1, r],
            {"exp": ((y + dy) % Y) * 2 + c},
        )

    def scopy(dy, r, owner):
        rows = block_rows(owner, r)
        return remote(
            xall.at[rows], xall.at[rows], ss.at[dy, r], sr.at[dy, r], {"exp": sib}
        )

    for r in range(ROWCH):
        part = slice(r * RC, (r + 1) * RC)
        inv = lax.rsqrt(jnp.sum(sq[part], axis=-1, keepdims=True) / D + 1e-06)
        xall[block_rows(me_e, r)] = (rs[part].astype(F32) * inv * ng[...]).astype(BF)
        for dy in range(1, Y):
            ycopy(dy, r, me_e).start()
        scopy(0, r, me_e).start()

    def from_y(dy):
        return (y + Y - dy) % Y

    def gates(yy):
        for l in range(L):
            for b in range(2):
                gt = gall[yy * 2 + b].T
                pick = lax.broadcasted_iota(jnp.int32, (T, EXPERTS), 1) == me_e * L + l
                col = jnp.sum(jnp.where(pick, gt, 0.0), axis=1, keepdims=True)
                gc[l, b * T : (b + 1) * T] = jnp.broadcast_to(col, (T, HD))

    def act(gp, up, gate):
        return (0.5 * gp * (1.0 + jnp.tanh(0.5 * gp)) * up * gate).astype(BF)

    def gate_up(yy, first):
        rows = pl.ds(pl.multiple_of(yy * 2 * T, 2 * T), 2 * T)
        for l in range(L):
            if first:
                wcopies[2 * l].wait()
                wcopies[2 * l + 1].wait()

            def body(j, carry):
                cols = pl.ds(pl.multiple_of(j * FT, FT), FT)
                xv = xall[rows]
                gp = dot(xv, wgv[l, :, cols])
                up = dot(xv, wuv[l, :, cols])
                gate = jnp.concatenate([gc[l]] * (FT // HD), axis=1)
                hid[:, pl.ds(pl.multiple_of(l * FF + j * FT, HD), FT)] = act(gp, up, gate)
                return carry

            full = FF // FT
            lax.fori_loop(0, full, body, 0)
            tail = FF - full * FT
            if tail:
                w = jnp.concatenate([wgv[l, :, full * FT :], wuv[l, :, full * FT :]], axis=1)
                o = dot(xall[rows], w)
                gate = jnp.concatenate([gc[l]] * (tail // HD), axis=1)
                hid[:, l * FF + full * FT : (l + 1) * FF] = act(o[:, :tail], o[:, tail:], gate)

    own = pl.ds(pl.multiple_of(c * T, T), T)
    other = pl.ds(pl.multiple_of((1 - c) * T, T), T)

    def lcopy(j):
        return remote(lsb.at[j], lrb.at[j], ls.at[j], lr.at[j], {"exp": sib})

    def pcopy(dy, j):
        return remote(
            rsb.at[dy - 1, j], rrb.at[dy - 1, j], ps.at[dy - 1, j], pr.at[dy - 1, j],
            {"exp": sib},
        )

    def bcopy(dy, j):
        return remote(
            ysb.at[dy - 1, j], yrb.at[dy - 1, j], bs.at[dy - 1, j], br.at[dy - 1, j],
            {"exp": from_y(dy) * 2 + c},
        )

    def tile_of(j):
        return pl.ds(pl.multiple_of(j * TN, TN), TN)

    for d in range(1, n_exp):
        gcopy(d, (me_e + n_exp - d) % n_exp).wait_recv()
    gates(y)
    for r in range(ROWCH):
        scopy(0, r, sib).wait_recv()
    gate_up(y, True)

    def forward(dy, r):
        owner = from_y(dy) * 2 + c
        ycopy(dy, r, owner).wait_recv()
        scopy(dy, r, owner).start()

    for dy in range(1, Y):
        forward(dy, 0)
    for l in range(L):
        wcopies[2 * L + l].wait()

    def local_down(j, carry):
        cols = tile_of(j)
        to[...] = dot(hid[...], wdv[:, cols])
        lsb[j] = to[other].astype(BF)
        lcopy(j).start()
        acc[:, cols] = to[own] + rs[:, cols].astype(F32)
        return carry

    lax.fori_loop(0, NT, local_down, 0)

    for dy in range(1, Y):
        for r in range(1, ROWCH):
            forward(dy, r)
        gates(from_y(dy))
        for r in range(ROWCH):
            scopy(dy, r, from_y(dy) * 2 + 1 - c).wait_recv()
        gate_up(from_y(dy), False)

        def combine(j):
            pcopy(dy, j).wait_recv()
            ysb[dy - 1, j] = (rown[j % 2] + rrb[dy - 1, j].astype(F32)).astype(BF)
            bcopy(dy, j).start()

        def remote_down(j, carry):
            to[...] = dot(hid[...], wdv[:, tile_of(j)])
            rsb[dy - 1, j] = to[other].astype(BF)
            pcopy(dy, j).start()
            rown[j % 2] = to[own]

            @pl.when(j > 0)
            def _():
                combine(j - 1)

            return carry

        lax.fori_loop(0, NT, remote_down, 0)
        combine(NT - 1)

    def add_local(j, carry):
        lcopy(j).wait_recv()
        acc[:, tile_of(j)] += lrb[j].astype(F32)
        return carry

    lax.fori_loop(0, NT, add_local, 0)

    def final(j, carry):
        cols = tile_of(j)
        a = acc[:, cols]
        for dy in range(1, Y):
            bcopy(dy, j).wait_recv()
            a = a + yrb[dy - 1, j].astype(F32)
        out[:, cols] = a.astype(BF)
        return carry

    lax.fori_loop(0, NT, final, 0)

    for d in range(1, n_exp):
        gcopy(d, me_e).wait_send()

    def sent_states(i, carry):
        for d in range(1, X):
            xcopy(d, i).wait_send()

        @pl.when(z < Z - 1)
        def _():
            zcopy(i).wait_send()

        return carry

    lax.fori_loop(0, NCH, sent_states, 0)
    for r in range(ROWCH):
        scopy(0, r, me_e).wait_send()
        for dy in range(1, Y):
            ycopy(dy, r, me_e).wait_send()
            scopy(dy, r, from_y(dy) * 2 + c).wait_send()

    def sent_parts(j, carry):
        lcopy(j).wait_send()
        for dy in range(1, Y):
            pcopy(dy, j).wait_send()
            bcopy(dy, j).wait_send()
        return carry

    lax.fori_loop(0, NT, sent_parts, 0)


def on_device(
    n_seq, n_exp,
    residual_in, query_matrix, key_vectors, value_vectors, head_gain, norm_gain,
    expert_ids, gate_probs, w_gate, w_up, w_down,
):
    T, D = residual_in.shape[1:]
    L, _, FF = w_gate.shape
    X = max(1, n_seq // 4)
    Y = n_exp // 2
    NT = D // TN
    cfg = (n_seq, n_exp, X, L, T, D, FF)
    DMA = pltpu.SemaphoreType.DMA
    vm = pl.BlockSpec(memory_space=pltpu.VMEM)
    anyspace = pl.BlockSpec(memory_space=pl.ANY)
    V = pltpu.VMEM
    y1 = max(1, Y - 1)
    x1 = max(1, X - 1)
    out = pl.pallas_call(
        functools.partial(kernel, cfg),
        out_shape=jax.ShapeDtypeStruct((T, D), BF),
        in_specs=[vm] * 8 + [anyspace] * 3,
        out_specs=vm,
        scratch_shapes=[
            V((HEADS, HD, HD), F32),
            V((HEADS, HD, HD), BF),
            V((x1, HEADS, HD, HD), BF),
            V((HEADS, HD, HD), BF),
            V((HEADS, HD, HD), BF),
            V((T, D), F32),
            V((T, D), BF),
            V((T, HD), F32),
            V((n_exp, EXPERTS, T), F32),
            V((n_exp * T, D), BF),
            V((L, D, FF), BF),
            V((L, D, FF), BF),
            V((L * FF, D), BF),
            V((2 * T, L * FF), BF),
            V((L, 2 * T, HD), F32),
            V((2 * T, TN), F32),
            V((NT, T, TN), BF),
            V((NT, T, TN), BF),
            V((y1, NT, T, TN), BF),
            V((y1, NT, T, TN), BF),
            V((2, T, TN), F32),
            V((y1, NT, T, TN), BF),
            V((y1, NT, T, TN), BF),
            DMA((3 * L,)),
            DMA((n_exp - 1,)),
            DMA((n_exp - 1,)),
            DMA((x1, NCH)),
            DMA((x1, NCH)),
            DMA((NCH,)),
            DMA((NCH,)),
            DMA((y1, ROWCH)),
            DMA((y1, ROWCH)),
            DMA((Y, ROWCH)),
            DMA((Y, ROWCH)),
            DMA((NT,)),
            DMA((NT,)),
            DMA((y1, NT)),
            DMA((y1, NT)),
            DMA((y1, NT)),
            DMA((y1, NT)),
        ],
        compiler_params=pltpu.CompilerParams(
            collective_id=0, has_side_effects=True, vmem_limit_bytes=63 * 1024 * 1024
        ),
        cost_estimate=pl.CostEstimate(
            flops=2 * n_exp * T * L * D * FF * 3, bytes_accessed=6 * L * D * FF, transcendentals=0
        ),
    )(
        residual_in[0], query_matrix[0], key_vectors[0], value_vectors[0],
        head_gain[None], norm_gain[None], expert_ids[0], gate_probs[0],
        w_gate, w_up, w_down.reshape(L * FF, D),
    )
    return out[None]


def solution(mesh):
    rows = P("exp", "seq", None)
    experts = P("exp", None, None)
    in_specs = (rows, rows, rows, rows, P(), P(), rows, rows, experts, experts, experts)
    return jax.shard_map(
        functools.partial(on_device, mesh.shape["seq"], mesh.shape["exp"]),
        mesh=mesh, in_specs=in_specs, out_specs=rows, check_vma=False,
    )
```

time: 419 us -> 104 us (0.25); the launches traced: 415 us -> 104 us
  waiting for transfers between devices: 185 us -> 0 us
  Pallas kernels: 0 us -> 98.5 us
  blocking collectives: 74.6 us -> 0 us
  local copies, waits for them, and re-layouts: 61.9 us -> 5.26 us
  matrix products: 48.9 us -> 0 us
  other arithmetic: 25.2 us -> 0 us
  between operations: 13.6 us -> 0.01 us
  starting transfers between devices: 5.63 us -> 0 us
    all_gather x1 -> x0, waiting for transfers between devices: 116 us -> none  [on_device(): piece = lax.all_gather(state[None], 'seq', axis=0, tiled=True)]
    pallas_call x0 -> x1, Pallas kernels: none -> 98.5 us  [on_device(): pl.pallas_call(functools.partial(kernel, cfg), out_shape=jax.ShapeDtypeSt...]
    all_to_all x1 -> x0, blocking collectives: 74.6 us -> none  [on_device(): lax.all_to_all(outgoing, 'exp', split_axis=0, concat_axis=0, tiled=True)]
    all_to_all x1 -> x0, waiting for transfers between devices: 68.4 us -> none  [on_device(): lax.all_to_all(result, 'exp', split_axis=0, concat_axis=0, tiled=True)]
    dot_general x5 -> x0, matrix products: 48.9 us -> none  [the longest x1 28 us: on_device(): jnp.einsum('genf,efd->gend', hidden, w_down, preferred_element_type=jnp.f...]
    scatter x1 -> x0, local copies, waits for them, and re-layouts: 22.9 us -> none  [on_device(): outgoing = jnp.zeros((EXPERTS * CAP, D), jnp.bfloat16).at[target].set(nor...]
    reduce_sum x4 -> x0, other arithmetic: 18.1 us -> none  [the longest x1 11.5 us: on_device(): jnp.sum(picked.astype(jnp.float32) * route_gates[:, :, None], axis=1)]
    convert_element_type x2 -> x0, local copies, waits for them, and re-layouts: 14.8 us -> none  [the longest x1 8.31 us: on_device(): picked.astype(jnp.float32) * route_gates[:, :, None]]
  transfers between devices with their start and end apart: 2 -> 0, of which waited for: 2 -> 0; matrix products, arithmetic and copies ran while one was open for 2% -> 0% of each run, Pallas kernels for 0% -> 0%
where the time goes in v1:
time: 104 us
  Pallas kernels  98.5 us (95%)
  local copies, waits for them, and re-layouts  5.26 us (5%)
    pallas_call x1, Pallas kernels, on_device(): pl.pallas_call(functools.partial(kernel, cfg), out_shape=jax.ShapeDtypeSt...  98.5 us
    unnamed x3, local copies, waits for them, and re-layouts  5.26 us

profile of v1, /device:TPU:24, one launch (start us, length us, event | category | flops | bytes accessed | tf_op | source)
XLA Modules:
  0.0 103.8 jit_solution(8584233436400076319)
XLA Ops:
  0.0 1.5 %copy.12 = s32[1,256,4]{2,1,0:T(8,128)} copy(s32[1,256,4]{1,2,0:T(4,128)} %param.17) | data formatting | bytes 8192 | tf_op args[6]
  1.5 1.5 %copy.13 = f32[1,256,4]{2,1,0:T(8,128)} copy(f32[1,256,4]{1,2,0:T(4,128)} %param.18) | data formatting | bytes 8192 | tf_op args[7]
  3.0 98.5 %shard_map.109 = bf16[256,2048]{1,0:T(8,128)(2,1)} custom-call(bf16[256,2048]{1,0:T(8,128)(2,1)} %bitcast.14, bf16[256,2048]{1,0:T(8,128)(2,1)} %bitcast.15, bf16[256,2048]{1,0:T(8,128)(2,1)} %bitcast.16, bf16[256,2048]{1,0:T(8,128)(2,1)} %bitcast.17, f32[1,2048]{1,0:T(1,128)} %bitcast.18, f32[1,2048]{1,0:T(1,128)} %bitcast.19, s32[256,4]{1,0:T(8,128)} %bitcast.11, ...), custom_call_target="tpu_custom_call" | custom-call | flops 35433480192 | bytes 34603008 | tf_op jit(solution)/shard_map/pallas_call | solution.py:396
  101.5 2.3 %copy.15 = bf16[1,256,2048]{2,1,0:T(8,128)(2,1)} copy(bf16[1,256,2048]{2,1,0:T(8,128)(2,1)} %bitcast.10) | data formatting | bytes 2097152

commit v2 on v1

--- a/solution.py
+++ b/solution.py
@@ -73,11 +73,11 @@
     for w in wcopies:
         w.start()
 
-    lane = lax.broadcasted_iota(jnp.int32, (T, HD), 1)
-    g = jnp.zeros((T, HD), F32)
-    for t in range(ids.shape[1]):
-        g = g + jnp.where(lane == ids[:, t : t + 1], probs[:, t : t + 1], 0.0)
-    gall[me_e] = g.T[:EXPERTS]
+    expert = lax.broadcasted_iota(jnp.int32, (EXPERTS, T), 0)
+    g = jnp.zeros((EXPERTS, T), F32)
+    for t in range(ids.shape[0]):
+        g = g + jnp.where(expert == ids[t : t + 1], probs[t : t + 1], 0.0)
+    gall[me_e] = g
 
     @pl.when(z == 0)
     def _():
@@ -190,7 +190,7 @@
     RC = T // ROWCH
 
     def block_rows(owner, r):
-        return pl.ds(pl.multiple_of(owner * T + r * RC, RC), RC)
+        return pl.ds(pl.multiple_of(((owner // 2 * ROWCH + r) * 2 + owner % 2) * RC, RC), RC)
 
     def ycopy(dy, r, owner):
         rows = block_rows(owner, r)
@@ -222,13 +222,17 @@
                 gt = gall[yy * 2 + b].T
                 pick = lax.broadcasted_iota(jnp.int32, (T, EXPERTS), 1) == me_e * L + l
                 col = jnp.sum(jnp.where(pick, gt, 0.0), axis=1, keepdims=True)
-                gc[l, b * T : (b + 1) * T] = jnp.broadcast_to(col, (T, HD))
+                for r in range(ROWCH):
+                    at = (r * 2 + b) * RC
+                    gc[l, at : at + RC] = jnp.broadcast_to(col[r * RC : (r + 1) * RC], (RC, HD))
 
     def act(gp, up, gate):
         return (0.5 * gp * (1.0 + jnp.tanh(0.5 * gp)) * up * gate).astype(BF)
 
-    def gate_up(yy, first):
-        rows = pl.ds(pl.multiple_of(yy * 2 * T, 2 * T), 2 * T)
+    def gate_up(yy, r0, count, first):
+        M = count * 2 * RC
+        rows = pl.ds(pl.multiple_of((yy * ROWCH + r0) * 2 * RC, 2 * RC), M)
+        grows = slice(r0 * 2 * RC, r0 * 2 * RC + M)
         for l in range(L):
             if first:
                 wcopies[2 * l].wait()
@@ -239,8 +243,8 @@
                 xv = xall[rows]
                 gp = dot(xv, wgv[l, :, cols])
                 up = dot(xv, wuv[l, :, cols])
-                gate = jnp.concatenate([gc[l]] * (FT // HD), axis=1)
-                hid[:, pl.ds(pl.multiple_of(l * FF + j * FT, HD), FT)] = act(gp, up, gate)
+                gate = jnp.concatenate([gc[l, grows]] * (FT // HD), axis=1)
+                hid[:M, pl.ds(pl.multiple_of(l * FF + j * FT, HD), FT)] = act(gp, up, gate)
                 return carry
 
             full = FF // FT
@@ -249,11 +253,11 @@
             if tail:
                 w = jnp.concatenate([wgv[l, :, full * FT :], wuv[l, :, full * FT :]], axis=1)
                 o = dot(xall[rows], w)
-                gate = jnp.concatenate([gc[l]] * (tail // HD), axis=1)
-                hid[:, l * FF + full * FT : (l + 1) * FF] = act(o[:, :tail], o[:, tail:], gate)
-
-    own = pl.ds(pl.multiple_of(c * T, T), T)
-    other = pl.ds(pl.multiple_of((1 - c) * T, T), T)
+                gate = jnp.concatenate([gc[l, grows]] * (tail // HD), axis=1)
+                hid[:M, l * FF + full * FT : (l + 1) * FF] = act(o[:, :tail], o[:, tail:], gate)
+
+    def half(r, core):
+        return pl.ds(pl.multiple_of((r * 2 + core) * RC, RC), RC)
 
     def lcopy(j):
         return remote(lsb.at[j], lrb.at[j], ls.at[j], lr.at[j], {"exp": sib})
@@ -278,7 +282,7 @@
     gates(y)
     for r in range(ROWCH):
         scopy(0, r, sib).wait_recv()
-    gate_up(y, True)
+    gate_up(y, 0, ROWCH, True)
 
     def forward(dy, r):
         owner = from_y(dy) * 2 + c
@@ -293,40 +297,44 @@
     def local_down(j, carry):
         cols = tile_of(j)
         to[...] = dot(hid[...], wdv[:, cols])
-        lsb[j] = to[other].astype(BF)
+        for r in range(ROWCH):
+            lsb[j, r * RC : (r + 1) * RC] = to[half(r, 1 - c)].astype(BF)
         lcopy(j).start()
-        acc[:, cols] = to[own] + rs[:, cols].astype(F32)
+        for r in range(ROWCH):
+            part = slice(r * RC, (r + 1) * RC)
+            acc[part, cols] = to[half(r, c)] + rs[part, cols].astype(F32)
         return carry
 
     lax.fori_loop(0, NT, local_down, 0)
 
     for dy in range(1, Y):
-        for r in range(1, ROWCH):
-            forward(dy, r)
         gates(from_y(dy))
         for r in range(ROWCH):
             scopy(dy, r, from_y(dy) * 2 + 1 - c).wait_recv()
-        gate_up(from_y(dy), False)
-
-        def combine(j):
-            pcopy(dy, j).wait_recv()
-            ysb[dy - 1, j] = (rown[j % 2] + rrb[dy - 1, j].astype(F32)).astype(BF)
-            bcopy(dy, j).start()
-
-        def remote_down(j, carry):
-            to[...] = dot(hid[...], wdv[:, tile_of(j)])
-            rsb[dy - 1, j] = to[other].astype(BF)
-            pcopy(dy, j).start()
-            rown[j % 2] = to[own]
-
-            @pl.when(j > 0)
-            def _():
-                combine(j - 1)
-
-            return carry
-
-        lax.fori_loop(0, NT, remote_down, 0)
-        combine(NT - 1)
+            gate_up(from_y(dy), r, 1, False)
+            if r + 1 < ROWCH:
+                forward(dy, r + 1)
+
+            def combine(j, i):
+                pcopy(dy, i).wait_recv()
+                ysb[dy - 1, i] = (rown[j % 2] + rrb[dy - 1, i].astype(F32)).astype(BF)
+                bcopy(dy, i).start()
+
+            def remote_down(j, carry):
+                i = r * NT + j
+                to[: 2 * RC] = dot(hid[: 2 * RC], wdv[:, tile_of(j)])
+                rsb[dy - 1, i] = to[half(0, 1 - c)].astype(BF)
+                pcopy(dy, i).start()
+                rown[j % 2] = to[half(0, c)]
+
+                @pl.when(j > 0)
+                def _():
+                    combine(j - 1, i - 1)
+
+                return carry
+
+            lax.fori_loop(0, NT, remote_down, 0)
+            combine(NT - 1, r * NT + NT - 1)
 
     def add_local(j, carry):
         lcopy(j).wait_recv()
@@ -336,15 +344,16 @@
     lax.fori_loop(0, NT, add_local, 0)
 
     def final(j, carry):
-        cols = tile_of(j)
-        a = acc[:, cols]
+        cols = tile_of(j % NT)
+        part = pl.ds(pl.multiple_of(j // NT * RC, RC), RC)
+        a = acc[part, cols]
         for dy in range(1, Y):
             bcopy(dy, j).wait_recv()
             a = a + yrb[dy - 1, j].astype(F32)
-        out[:, cols] = a.astype(BF)
-        return carry
-
-    lax.fori_loop(0, NT, final, 0)
+        out[part, cols] = a.astype(BF)
+        return carry
+
+    lax.fori_loop(0, ROWCH * NT, final, 0)
 
     for d in range(1, n_exp):
         gcopy(d, me_e).wait_send()
@@ -367,13 +376,14 @@
             scopy(dy, r, from_y(dy) * 2 + c).wait_send()
 
     def sent_parts(j, carry):
-        lcopy(j).wait_send()
         for dy in range(1, Y):
             pcopy(dy, j).wait_send()
             bcopy(dy, j).wait_send()
         return carry
 
-    lax.fori_loop(0, NT, sent_parts, 0)
+    lax.fori_loop(0, ROWCH * NT, sent_parts, 0)
+    for j in range(NT):
+        lcopy(j).wait_send()
 
 
 def on_device(
@@ -417,11 +427,11 @@
             V((2 * T, TN), F32),
             V((NT, T, TN), BF),
             V((NT, T, TN), BF),
-            V((y1, NT, T, TN), BF),
-            V((y1, NT, T, TN), BF),
-            V((2, T, TN), F32),
-            V((y1, NT, T, TN), BF),
-            V((y1, NT, T, TN), BF),
+            V((y1, ROWCH * NT, T // ROWCH, TN), BF),
+            V((y1, ROWCH * NT, T // ROWCH, TN), BF),
+            V((2, T // ROWCH, TN), F32),
+            V((y1, ROWCH * NT, T // ROWCH, TN), BF),
+            V((y1, ROWCH * NT, T // ROWCH, TN), BF),
             DMA((3 * L,)),
             DMA((n_exp - 1,)),
             DMA((n_exp - 1,)),
@@ -435,10 +445,10 @@
             DMA((Y, ROWCH)),
             DMA((NT,)),
             DMA((NT,)),
-            DMA((y1, NT)),
-            DMA((y1, NT)),
-            DMA((y1, NT)),
-            DMA((y1, NT)),
+            DMA((y1, ROWCH * NT)),
+            DMA((y1, ROWCH * NT)),
+            DMA((y1, ROWCH * NT)),
+            DMA((y1, ROWCH * NT)),
         ],
         compiler_params=pltpu.CompilerParams(
             collective_id=0, has_side_effects=True, vmem_limit_bytes=63 * 1024 * 1024
@@ -448,7 +458,7 @@
         ),
     )(
         residual_in[0], query_matrix[0], key_vectors[0], value_vectors[0],
-        head_gain[None], norm_gain[None], expert_ids[0], gate_probs[0],
+        head_gain[None], norm_gain[None], expert_ids[0].T, gate_probs[0].T,
         w_gate, w_up, w_down.reshape(L * FF, D),
     )
     return out[None]

time: 104 us -> 94.6 us (0.910)
  Pallas kernels: 98.5 us -> 92.2 us
  local copies, waits for them, and re-layouts: 5.26 us -> 2.3 us
    pallas_call x1, Pallas kernels: 98.5 us -> 92.2 us  [on_device(): pl.pallas_call(functools.partial(kernel, cfg), out_shape=jax.ShapeDtypeSt...]
    unnamed x3 -> x1, local copies, waits for them, and re-layouts: 5.26 us -> 2.3 us
where the time goes in v2:
time: 94.6 us; the launch traced here: 94.5 us
  Pallas kernels  92.2 us (97%)
  local copies, waits for them, and re-layouts  2.3 us (2%)
    pallas_call x1, Pallas kernels, on_device(): pl.pallas_call(functools.partial(kernel, cfg), out_shape=jax.ShapeDtypeSt...  92.2 us
    unnamed x1, local copies, waits for them, and re-layouts  2.3 us

profile of v2, /device:TPU:24, one launch (start us, length us, event | category | flops | bytes accessed | tf_op | source)
XLA Modules:
  0.0 94.5 jit_solution(3002138872416658593)
XLA Ops:
  0.0 92.2 %shard_map.109 = bf16[256,2048]{1,0:T(8,128)(2,1)} custom-call(bf16[256,2048]{1,0:T(8,128)(2,1)} %bitcast.16, bf16[256,2048]{1,0:T(8,128)(2,1)} %bitcast.17, bf16[256,2048]{1,0:T(8,128)(2,1)} %bitcast.18, bf16[256,2048]{1,0:T(8,128)(2,1)} %bitcast.19, f32[1,2048]{1,0:T(1,128)} %bitcast.20, f32[1,2048]{1,0:T(1,128)} %bitcast.21, s32[4,256]{1,0:T(4,128)} %bitcast.22, ...), custom_call_target="tpu_custom_call" | custom-call | flops 35433480192 | bytes 34603008 | tf_op jit(solution)/shard_map/pallas_call | solution.py:406
  92.2 2.3 %copy.13 = bf16[1,256,2048]{2,1,0:T(8,128)(2,1)} copy(bf16[1,256,2048]{2,1,0:T(8,128)(2,1)} %bitcast.14) | data formatting | bytes 2097152

commit v3 on v2

--- a/solution.py
+++ b/solution.py
@@ -150,7 +150,9 @@
             acc[:, cols] = dot(w, v[:, cols])
         return carry
 
-    lax.fori_loop(0, NCH, inner_body, 0)
+    @pl.when(z > 0)
+    def _():
+        lax.fori_loop(0, NCH, inner_body, 0)
 
     def chain_body(i, carry):
         sl = pl.ds(i * CH, CH)
@@ -172,6 +174,10 @@
         def _():
             zo[sl] = (p + t).astype(BF)
             zcopy(i).start()
+
+        @pl.when(z == 0)
+        def _():
+            inner_body(i, 0)
 
         pf = (p + before).astype(BF)
         for hh in range(CH):

time: 94.6 us -> 92.3 us (0.976)
  Pallas kernels: 92.2 us -> 89.8 us
    pallas_call x1, Pallas kernels: 92.2 us -> 89.8 us  [on_device(): pl.pallas_call(functools.partial(kernel, cfg), out_shape=jax.ShapeDtypeSt...]
where the time goes in v3:
time: 92.3 us; the launch traced here: 92.1 us
  Pallas kernels  89.8 us (97%)
  local copies, waits for them, and re-layouts  2.3 us (2%)
    pallas_call x1, Pallas kernels, on_device(): pl.pallas_call(functools.partial(kernel, cfg), out_shape=jax.ShapeDtypeSt...  89.8 us
    unnamed x1, local copies, waits for them, and re-layouts  2.3 us

profile of v3, /device:TPU:24, one launch (start us, length us, event | category | flops | bytes accessed | tf_op | source)
XLA Modules:
  0.0 92.1 jit_solution(18360143653024239168)
XLA Ops:
  0.0 89.8 %shard_map.109 = bf16[256,2048]{1,0:T(8,128)(2,1)} custom-call(bf16[256,2048]{1,0:T(8,128)(2,1)} %bitcast.16, bf16[256,2048]{1,0:T(8,128)(2,1)} %bitcast.17, bf16[256,2048]{1,0:T(8,128)(2,1)} %bitcast.18, bf16[256,2048]{1,0:T(8,128)(2,1)} %bitcast.19, f32[1,2048]{1,0:T(1,128)} %bitcast.20, f32[1,2048]{1,0:T(1,128)} %bitcast.21, s32[4,256]{1,0:T(4,128)} %bitcast.22, ...), custom_call_target="tpu_custom_call" | custom-call | flops 35433480192 | bytes 34603008 | tf_op jit(solution)/shard_map/pallas_call | solution.py:412
  89.8 2.3 %copy.13 = bf16[1,256,2048]{2,1,0:T(8,128)(2,1)} copy(bf16[1,256,2048]{2,1,0:T(8,128)(2,1)} %bitcast.14) | data formatting | bytes 2097152
